TPU v7x, 512 devices: a whole 4x4x16 slice. The times are simulated.
512 devices in a mesh: mirror: 32 (over z, y_hi), request: 8 (over x, y_lo), tensor: 2 (over core).
Axes of the slice: x: 4, y: 4 (y_hi: 2, y_lo: 2; y = y_hi * 2 + y_lo), z: 16, core: 2. Of those that a mesh axis runs over, the one named last changes fastest.
Arguments:
- k_cache: bfloat16 [256, 256, 512], P(('request', 'mirror'), None, 'tensor'), parts along dimension 0, may hold values from -12 to 12
- value_cache: bfloat16 [256, 256, 512], P(('request', 'mirror'), None, 'tensor'), parts along dimension 0, may hold values from -6 to 6
- recomputed_queries: bfloat16 [256, 128, 4096], P(('request', 'mirror'), None, 'tensor'), parts along dimension 0, may hold values from -36 to 36
- recomputed_keys: bfloat16 [256, 128, 512], P(('request', 'mirror'), None, 'tensor'), parts along dimension 0, may hold values from -6 to 6
- recomputed_values: bfloat16 [256, 128, 512], P(('request', 'mirror'), None, 'tensor'), parts along dimension 0, may hold values from -6 to 6
- sel_index: int32 [256, 128], P('request'), parts along dimension 0, may hold values from 0 to 255, as said below
- counts: int32 [256], P('request'), parts along dimension 0, may hold values from 48 to 128
- span_order: int32 [256], P('request'), parts along dimension 0, may hold values from 0 to 31, each once
Outputs:
- attn_out: bfloat16 [256, 128, 4096], P(('request', 'mirror'), None, 'tensor'), parts along dimension 0
- mixed_keys: bfloat16 [256, 256, 512], P(('request', 'mirror'), None, 'tensor'), parts along dimension 0
- mixed_values: bfloat16 [256, 256, 512], P(('request', 'mirror'), None, 'tensor'), parts along dimension 0
- deviation: float32 [256, 128], P(('request', 'mirror')), parts along dimension 0
There are 8 independent parts, one for each index of `request`. A program takes and returns all parts, laid end to end along the dimension named above; each array names one. Nothing has to cross between parts.
Inputs may be any that keep to these rules, and one draw needn't show every extreme that they name: `sel_index`: for slot s the first counts[s] entries are distinct increasing token positions of span span_order[s]; the other entries are 0. `span_order`: a permutation of the span numbers.
All inputs are finite; a program needn't handle non-finite values.
Results may differ from a plain program's by a relative error of at most 0.0085.
Values may be sent and summed in bfloat16 or wider, within the bound.
A program may use at most 64 MiB of HBM per device.

v0:
```python
import math

import jax
import jax.numpy as jnp
from jax import lax
from jax.sharding import PartitionSpec as P

HEAD_DIMENSION = 128


large_negative = -1e30


def pick_entry(lookup, where_at):
    spots = jnp.arange(lookup.shape[0], dtype=jnp.int32)
    return jnp.sum(jnp.where(spots == where_at, lookup, jnp.zeros_like(lookup)))


def pick_row(lookup, where_at):
    return lax.dynamic_index_in_dim(lookup, where_at, 0, keepdims=False)


def absorb(carry_state, query_block, key_row_block, value_row_block, allowed, needed, scaling):

    def update(current):
        highest, totals, summed = current
        scores = (
            jnp.einsum(
                "rhgd,khd->hgrk", query_block, key_row_block, preferred_element_type=jnp.float32
            )
            * scaling
        )
        scores = jnp.where(allowed, scores, large_negative)
        new_high = jnp.maximum(highest, jnp.max(scores, axis=-1))
        weights = jnp.where(allowed, jnp.exp(scores - new_high[..., None]), 0.0)
        decay_factor = jnp.exp(highest - new_high)
        totals = totals * decay_factor + jnp.sum(weights, axis=-1)
        summed = summed * decay_factor[..., None] + jnp.einsum(
            "hgrk,khd->hgrd",
            weights.astype(jnp.bfloat16),
            value_row_block,
            preferred_element_type=jnp.float32,
        )
        return (new_high, totals, summed)

    return lax.cond(needed, update, lambda current: current, carry_state)


def blend_rows(cached, incoming, tokens, live_rows):
    places = jnp.arange(cached.shape[0], dtype=jnp.int32)
    matched = (places[:, None] == tokens[None, :]) & live_rows[None, :]
    markers = matched.astype(jnp.bfloat16)
    moved = jnp.dot(markers, incoming, preferred_element_type=jnp.float32).astype(jnp.bfloat16)
    return (jnp.where(jnp.any(matched, axis=1)[:, None], moved, cached), markers)


def finish(carry_state, live_rows):
    highest, totals, summed = carry_state
    kv_heads, query_group_width, row_total, head_size = summed.shape
    result = (
        (summed / totals[..., None])
        .transpose(2, 0, 1, 3)
        .reshape(row_total, kv_heads * query_group_width * head_size)
    )
    return jnp.where(live_rows[:, None], result, 0.0).astype(jnp.bfloat16)


def key_deviation(markers, cached, incoming, live_rows):
    old_rows = jnp.dot(markers.T, cached, preferred_element_type=jnp.float32)
    gap = incoming.astype(jnp.float32) - old_rows
    partial_sums = jnp.sum(gap * gap, axis=1)
    summed_gap = lax.psum(partial_sums, "tensor")
    entries = cached.shape[1] * lax.axis_size("tensor")
    return jnp.where(live_rows, summed_gap / entries, 0.0)[None]


def body(
    k_cache,
    value_cache,
    recomputed_queries,
    recomputed_keys,
    recomputed_values,
    sel_index,
    counts,
    span_order,
):
    span_count, row_slots = sel_index.shape
    span_len = k_cache.shape[1]
    kv_cols = k_cache.shape[2]
    kv_heads = kv_cols // HEAD_DIMENSION
    query_group_width = recomputed_queries.shape[2] // kv_cols
    scaling = 1.0 / math.sqrt(HEAD_DIMENSION)
    my_index = lax.axis_index("mirror")
    slot_range = jnp.arange(span_count, dtype=jnp.int32)
    slot_of = jnp.sum(
        slot_range[:, None] * (span_order[:, None] == slot_range[None, :]).astype(jnp.int32), axis=0
    )
    live_table = jnp.arange(row_slots, dtype=jnp.int32)[None, :] < counts[:, None]
    my_slot = pick_entry(slot_of, my_index)
    places = jnp.arange(span_len, dtype=jnp.int32)
    queries_all = recomputed_queries[0].reshape(
        row_slots, kv_heads, query_group_width, HEAD_DIMENSION
    )
    own_tokens = pick_row(sel_index, my_index)
    own_live = pick_row(live_table, my_index)
    query_sets = ((queries_all, my_index, own_tokens),)

    def empty_state(query_rows):
        row_total = query_rows.shape[0]
        return (
            jnp.full((kv_heads, query_group_width, row_total), large_negative, jnp.float32),
            jnp.zeros((kv_heads, query_group_width, row_total), jnp.float32),
            jnp.zeros((kv_heads, query_group_width, row_total, HEAD_DIMENSION), jnp.float32),
        )

    states = tuple((empty_state(query_set[0]) for query_set in query_sets))

    def take_span(carried, span_number, key_row_block, value_row_block, excluded):
        slot_number = pick_entry(slot_of, span_number)
        key_row_block = key_row_block.reshape(span_len, kv_heads, HEAD_DIMENSION)
        value_row_block = value_row_block.reshape(span_len, kv_heads, HEAD_DIMENSION)
        updated = []
        for carry_state, query_set in zip(carried, query_sets):
            query_block, query_slot, query_tokens = query_set
            allowed = (
                (slot_number < query_slot) | (places[None, :] <= query_tokens[:, None])
            ) & jnp.logical_not(excluded)[None, :]
            updated.append(
                absorb(
                    carry_state,
                    query_block,
                    key_row_block,
                    value_row_block,
                    allowed,
                    slot_number <= query_slot,
                    scaling,
                )
            )
        return tuple(updated)

    def keep_own(kept, slot_number, key_row_block, value_row_block):
        chosen = slot_number == my_slot
        return (
            jnp.where(chosen, key_row_block, kept[0]),
            jnp.where(chosen, value_row_block, kept[1]),
        )

    blank = jnp.zeros((row_slots, kv_cols), jnp.bfloat16)
    my_tokens = pick_row(sel_index, my_slot)
    my_live = pick_row(live_table, my_slot)
    kept = (blank, blank)
    new_keys = lax.all_gather(recomputed_keys, "mirror", axis=0, tiled=True)
    new_values = lax.all_gather(recomputed_values, "mirror", axis=0, tiled=True)

    def step(inner, item):
        offset, new_k, new_v = item
        return (keep_own(inner, offset, new_k, new_v), None)

    offsets = jnp.arange(new_keys.shape[0], dtype=jnp.int32)
    kept, _ = lax.scan(step, kept, (offsets, new_keys, new_values))
    own_k, own_v = kept
    mixed_keys, markers = blend_rows(k_cache[0], own_k, my_tokens, my_live)
    mixed_values, _ = blend_rows(value_cache[0], own_v, my_tokens, my_live)
    deviation = key_deviation(markers, k_cache[0], own_k, my_live)
    no_rows = jnp.zeros((span_len,), jnp.bool_)
    carried = states
    blend_keys = lax.all_gather(mixed_keys[None], "mirror", axis=0, tiled=True)
    blend_values = lax.all_gather(mixed_values[None], "mirror", axis=0, tiled=True)

    def step(inner, item):
        offset, cache_k, cache_v = item
        return (take_span(inner, offset, cache_k, cache_v, no_rows), None)

    offsets = jnp.arange(blend_keys.shape[0], dtype=jnp.int32)
    carried, _ = lax.scan(step, carried, (offsets, blend_keys, blend_values))
    states = carried
    attn_out = finish(states[0], own_live)
    return (attn_out[None], mixed_keys[None], mixed_values[None], deviation)


def solution(mesh):
    in_specs = (
        P(("request", "mirror"), None, "tensor"),
        P(("request", "mirror"), None, "tensor"),
        P(("request", "mirror"), None, "tensor"),
        P(("request", "mirror"), None, "tensor"),
        P(("request", "mirror"), None, "tensor"),
        P("request", None),
        P("request"),
        P("request"),
    )
    out_specs = (
        P(("request", "mirror"), None, "tensor"),
        P(("request", "mirror"), None, "tensor"),
        P(("request", "mirror"), None, "tensor"),
        P(("request", "mirror"), None),
    )
    return jax.shard_map(body, mesh=mesh, in_specs=in_specs, out_specs=out_specs, check_vma=False)
```

profile of v0, /device:TPU:504, one launch (start us, length us, event | category | flops | bytes accessed | tf_op | source)
XLA Modules:
  0.0 934.8 jit_solution(18211062620991096580)
XLA Ops:
  13.7 142.7 %all-gather.7.cloned.1.call-done = bf16[32,128,256]{2,1,0:T(8,128)(2,1)} async-done(((bf16[1,128,256]{2,1,0:T(8,128)(2,1)}), bf16[32,128,256]{2,1,0:T(8,128)(2,1)}) %all-gather.7.cloned.1.call-update) | async-done | bytes 2097168 | tf_op jit(solution)/shard_map/all_gather | solution.py:152
  156.4 147.6 %all-gather.9.cloned.1.call-done = bf16[32,128,256]{2,1,0:T(8,128)(2,1)} async-done(((bf16[1,128,256]{2,1,0:T(8,128)(2,1)}), bf16[32,128,256]{2,1,0:T(8,128)(2,1)}) %all-gather.9.cloned.1.call-update) | async-done | bytes 2097168 | tf_op jit(solution)/shard_map/all_gather | solution.py:153
  304.0 90.5 %while.29 = (s32[]{:T(128)}, bf16[128,256]{1,0:T(8,128)(2,1)S(1)}, bf16[128,256]{1,0:T(8,128)(2,1)S(1)}, s32[32]{0:T(128)S(1)}, s32[]{:T(128)}, /*index=5*/bf16[...) while((s32[]{:T(128)}, bf16[128,256]{1,0:T(8,128)(2,1)S(1)}, ...), condition=%wide.region_4.5_spmd.clone, body=%wide.region_3.4_spmd.clone.sunk | while | flops 131076 | bytes 393353 | solution.py:160
  397.2 2.5 psum.7
  400.2 154.2 %all-gather.11.cloned.1.call-done = bf16[8192,256]{1,0:T(8,128)(2,1)} async-done(((bf16[256,256]{1,0:T(8,128)(2,1)}), bf16[8192,256]{1,0:T(8,128)(2,1)}) %all-gather.11.cloned.1.call-update) | async-done | bytes 4194320 | tf_op jit(solution)/shard_map/all_gather | solution.py:167
  554.4 6.5 copy.34
  560.8 155.8 %all-gather.13.cloned.1.call-done = bf16[8192,256]{1,0:T(8,128)(2,1)} async-done(((bf16[256,256]{1,0:T(8,128)(2,1)}), bf16[8192,256]{1,0:T(8,128)(2,1)}) %all-gather.13.cloned.1.call-update) | async-done | bytes 4194320 | tf_op jit(solution)/shard_map/all_gather | solution.py:168
  716.6 6.5 copy.36
  723.2 203.2 %while.28 = (s32[]{:T(128)}, f32[2,8,128]{2,1,0:T(8,128)S(1)}, f32[2,8,128]{2,1,0:T(8,128)S(1)}, f32[2,8,128,128]{3,2,1,0:T(8,128)S(1)}, s32[32]{0:T(128)S(1)}, ...) while((s32[]{:T(128)}, f32[2,8,128]{2,1,0:T(8,128)S(1)}, ...), condition=%wide.region_11.12_spmd.clone, body=%wide.region_5.11_spmd.clone.sunk | while | flops 275845216 | bytes 9964477 | solution.py:175
  723.8 1.3 fusion.40
  725.7 3.8 conditional.3
  730.2 1.3 fusion.40
  732.0 3.8 conditional.3
  736.5 1.3 fusion.40
  738.4 3.8 conditional.3
  742.9 1.3 fusion.40
  744.7 3.8 conditional.3
  749.2 1.3 fusion.40
  751.1 3.8 conditional.3
  755.6 1.3 fusion.40
  757.4 3.8 conditional.3
  761.9 1.3 fusion.40
  763.8 3.8 conditional.3
  768.3 1.3 fusion.40
  770.1 3.8 conditional.3
  774.6 1.3 fusion.40
  776.5 3.8 conditional.3
  782.8 3.8 conditional.3
  787.3 1.3 fusion.40
  789.2 3.8 conditional.3
  793.7 1.3 fusion.40
  795.5 3.8 conditional.3
  800.0 1.3 fusion.40
  801.9 3.8 conditional.3
  806.4 1.3 fusion.40
  808.2 3.8 conditional.3
  812.7 1.3 fusion.40
  814.6 3.8 conditional.3
  819.1 1.3 fusion.40
  820.9 3.8 conditional.3
  825.4 1.3 fusion.40
  827.3 3.8 conditional.3
  831.8 1.3 fusion.40
  833.6 3.8 conditional.3
  838.1 1.3 fusion.40
  840.0 3.8 conditional.3
  844.5 1.3 fusion.40
  846.3 3.8 conditional.3
  850.8 1.3 fusion.40
  852.7 3.8 conditional.3
  857.2 1.3 fusion.40
  859.0 3.8 conditional.3
  863.5 1.3 fusion.40
  865.4 3.8 conditional.3
  869.9 1.3 fusion.40
  871.7 3.8 conditional.3
  878.1 3.8 conditional.3
  884.4 3.8 conditional.3
  890.8 3.8 conditional.3
  897.1 3.8 conditional.3
  903.5 3.8 conditional.3
  909.8 3.8 conditional.3
  916.2 3.8 conditional.3
  922.5 3.8 conditional.3
  (430 shorter events, 193.3 us)
Async XLA Ops:
  7.2 387.4 %copy-start.2 = (bf16[1,256,256]{2,1,0:T(8,128)(2,1)S(1)}, bf16[1,256,256]{2,1,0:T(8,128)(2,1)}, u32[]{:S(2)}) copy-start(bf16[1,256,256]{2,1,0:T(8,128)(2,1)} %param.14) | copy-start | bytes 393220
  7.2 388.3 %copy-start.1 = (bf16[1,256,256]{2,1,0:T(8,128)(2,1)S(1)}, bf16[1,256,256]{2,1,0:T(8,128)(2,1)}, u32[]{:S(2)}) copy-start(bf16[1,256,256]{2,1,0:T(8,128)(2,1)} %param.15) | copy-start | bytes 393220
  7.2 389.1 %copy-start = (bf16[1,128,2048]{2,1,0:T(8,128)(2,1)S(1)}, bf16[1,128,2048]{2,1,0:T(8,128)(2,1)}, u32[]{:S(2)}) copy-start(bf16[1,128,2048]{2,1,0:T(8,128)(2,1)} %param.16) | copy-start | bytes 1572868
  7.2 149.2 %all-gather.7.cloned.1.call-start = ((), (), s32[]{:S(2)}) async-start(), calls=%async_computation | async-start | bytes 2162688 | tf_op jit(solution)/shard_map/all_gather | solution.py:152
  7.9 296.1 %all-gather.9.cloned.1.call-start = ((), (), s32[]{:S(2)}) async-start(), calls=%async_computation.1 | async-start | bytes 2162688 | tf_op jit(solution)/shard_map/all_gather | solution.py:153
  8.7 545.7 %all-gather.11.cloned.1.call-start = ((), (), s32[]{:S(2)}) async-start(), calls=%async_computation.2 | async-start | bytes 4325376 | tf_op jit(solution)/shard_map/all_gather | solution.py:167
  395.4 321.2 %all-gather.13.cloned.1.call-start = ((), (), s32[]{:S(2)}) async-start(), calls=%async_computation.3 | async-start | bytes 4325376 | tf_op jit(solution)/shard_map/all_gather | solution.py:168
Sparse Core Ops, SparseCore 0:
  11.1 145.1 all-gather.6
  159.5 144.4 all-gather.8
  395.5 158.7 all-gather.10
  557.9 158.6 all-gather.12
where the time goes:
time: 939 us; the launch traced here: 935 us
  waiting for transfers between devices  602 us (64%)
  other arithmetic  94.4 us (10%)
  local copies, waits for them, and re-layouts  86.5 us (9%)
  loops' own time  80.7 us (9%)
  matrix products  53 us (6%)
  between operations  15.8 us (2%)
    all_gather x1, waiting for transfers between devices, body(): lax.all_gather(mixed_values[None], 'mirror', axis=0, tiled=True)  156 us
    all_gather x1, waiting for transfers between devices, body(): blend_keys = lax.all_gather(mixed_keys[None], 'mirror', axis=0, tiled=True)  154 us
    all_gather x1, waiting for transfers between devices, body(): new_values = lax.all_gather(recomputed_values, 'mirror', axis=0, tiled=True)  148 us
    all_gather x1, waiting for transfers between devices, body(): new_keys = lax.all_gather(recomputed_keys, 'mirror', axis=0, tiled=True)  143 us
    another operation x1, loops' own time, body(): kept, _ = lax.scan(step, kept, (offsets, new_keys, new_values))  42.2 us
    reduce_sum x33, other arithmetic, pick_entry(): return jnp.sum(jnp.where(spots == where_at, lookup, jnp.zeros_like(lookup)))  41.3 us
    dynamic_slice x64, local copies, waits for them, and re-layouts, body(): kept, _ = lax.scan(step, kept, (offsets, new_keys, new_values))  39.6 us
    dot_general x32, matrix products, update(): jnp.einsum('hgrk,khd->hgrd', weights.astype(jnp.bfloat16), value_row_bloc...  34.4 us
  transfers between devices with their start and end apart: 4, of which 4 were waited for; matrix products, arithmetic and copies ran while one was open for 1% of the time, Pallas kernels for 0%

commit v1 on v0

v1 whole, which is shorter than its diff:
```python
import functools
import math

import jax
import jax.numpy as jnp
from jax import lax
from jax.experimental import pallas as pl
from jax.experimental.pallas import tpu as pltpu
from jax.sharding import PartitionSpec as P

HEAD = 128
TOKENS = 256
ROWS = 128
LEAST = 48
KEPT = TOKENS - LEAST
PART = KEPT + ROWS
PAD = 384
GROUP = 8
TILE = 256
LOW = -1e30
FAR = 1e9
SCALE = math.log2(math.e) / math.sqrt(HEAD)
F32 = jnp.float32
BF16 = jnp.bfloat16


def dot(a, b):
    return jnp.dot(a, b, preferred_element_type=F32)


def dot_nt(a, b):
    return lax.dot_general(a, b, (((1,), (1,)), ((), ())), preferred_element_type=F32)


def iota(shape, dim):
    return lax.broadcasted_iota(jnp.int32, shape, dim).astype(F32)


def turn(row):
    return jnp.broadcast_to(row, (ROWS, ROWS)).T


def kept_rows(sel_row, live):
    places = iota((ROWS, TOKENS), 1)
    side = turn(sel_row)
    side = jnp.concatenate([side, side], axis=1)
    slots = iota((ROWS, TOKENS), 0)
    hits = jnp.where((places == side) & (slots < live), 1.0, 0.0)
    keep = 1.0 - jnp.max(hits, axis=0, keepdims=True)
    before = jnp.where(iota((TOKENS, TOKENS), 0) < iota((TOKENS, TOKENS), 1), 1.0, 0.0)
    rank = dot(jnp.broadcast_to(keep, (8, TOKENS)).astype(BF16), before.astype(BF16))[:1]
    rank = jnp.where(keep > 0.5, rank, -1.0)
    return jnp.where(iota((PAD, TOKENS), 0) == rank, 1.0, 0.0).astype(BF16)


def kernel(
    levels,
    order_s,
    counts_s,
    k_ref,
    v_ref,
    q_ref,
    rk_ref,
    rv_ref,
    sel_ref,
    counts_ref,
    order_ref,
    out_ref,
    mk_ref,
    mv_ref,
    dev_ref,
    blocks,
    queries,
    acc,
    total,
    top,
    token_of,
    limit,
    away,
    rows_out,
    rows_in,
    answer,
    gap_mine,
    gap_other,
    block_recv,
    ring_send,
    away_send,
    query_send,
    query_recv,
    rows_send,
    rows_recv,
    answer_send,
    answer_recv,
    gap_send,
    gap_recv,
):
    spans = 2 * levels
    half_way = levels // 2
    last = levels - 1
    me = lax.axis_index("mirror")
    core = lax.axis_index("tensor")
    z, y = me // 2, me % 2
    partner = z * 2 + 1 - y
    up = ((z + 1) % levels) * 2 + y
    down = ((z + levels - 1) % levels) * 2 + y
    mine_at = pl.multiple_of(y * HEAD, HEAD)
    away_at = pl.multiple_of((1 - y) * HEAD, HEAD)
    mine_q = y * GROUP * HEAD
    away_q = (1 - y) * GROUP * HEAD

    barrier = pltpu.get_barrier_semaphore()
    for other in (up, down, partner):
        pl.semaphore_signal(barrier, inc=1, device_id={"mirror": other})
    pl.semaphore_signal(barrier, inc=1, device_id={"tensor": 1 - core})

    def send(src, dst, send_sem, recv_sem, to):
        return pltpu.make_async_remote_copy(
            src_ref=src, dst_ref=dst, send_sem=send_sem, recv_sem=recv_sem, device_id=to
        )

    def part(unit, kv, slot):
        return blocks.at[unit, kv, slot, pl.ds(0, PART), :]

    def ring(direction, src, unit, kv, slot, tag):
        to = {"mirror": up if direction == 0 else down}
        return send(
            src, part(unit, kv, slot), ring_send.at[direction, unit, tag],
            block_recv.at[unit, kv, slot], to,
        )

    def arrived(unit, kv, slot):
        send(
            part(unit, kv, slot), part(unit, kv, slot), ring_send.at[0, 0, 0],
            block_recv.at[unit, kv, slot], {"mirror": up},
        ).wait_recv()

    def find(s, found):
        return jnp.where(order_s[s] == me, s, found)

    my_slot = lax.fori_loop(0, spans, find, 0)
    my_live = counts_s[my_slot].astype(F32)
    sel_all = sel_ref[...].astype(F32)
    chosen = jnp.where(order_ref[...] == me, 1.0, 0.0)
    my_sel = dot(jnp.broadcast_to(chosen, (8, spans)).astype(BF16), sel_all.astype(BF16))[:1]

    keep_mine = kept_rows(my_sel, my_live)[:KEPT]
    for kv, (cache, fresh) in enumerate(((k_ref, rk_ref), (v_ref, rv_ref))):
        packed = dot(keep_mine, cache[:, pl.ds(mine_at, HEAD)]).astype(BF16)
        blocks[0, kv, 0, 0:KEPT, :] = packed
        blocks[0, kv, 0, KEPT:PART, :] = fresh[:, pl.ds(mine_at, HEAD)]
        packed = dot(keep_mine, cache[:, pl.ds(away_at, HEAD)]).astype(BF16)
        away[kv, 0:KEPT, :] = packed
        away[kv, KEPT:PART, :] = fresh[:, pl.ds(away_at, HEAD)]

    pl.semaphore_wait(barrier, 4)

    def across(kv):
        return send(
            away.at[kv], part(0, kv, 1), away_send.at[kv], block_recv.at[0, kv, 1],
            {"mirror": partner},
        )

    def ask(g):
        return send(
            q_ref.at[:, pl.ds(pl.multiple_of(away_q + g * HEAD, HEAD), HEAD)],
            queries.at[1, pl.ds(g * ROWS, ROWS), :],
            query_send.at[g], query_recv.at[g], {"mirror": partner},
        )

    for kv in range(2):
        across(kv).start()
        for direction in range(2):
            ring(direction, part(0, kv, 0), 1, kv, direction, kv).start()
    for g in range(GROUP):
        ask(g).start()

    counts_f = counts_ref[...].astype(F32)
    c_at, s_at = iota((spans, spans), 0), iota((spans, spans), 1)
    pick = order_ref[...].astype(F32) == c_at
    slot_of = jnp.sum(jnp.where(pick, s_at, 0.0), axis=1, keepdims=True)
    slot_live = jnp.sum(jnp.where(pick, counts_f, 0.0), axis=1, keepdims=True)
    row_live = jnp.sum(jnp.where(c_at == s_at, counts_f, 0.0), axis=1, keepdims=True)
    span_at = iota((spans, PAD), 0)[:, :1]
    lane = iota((spans, PAD), 1)
    for o, slot in ((0, me), (1, partner)):
        at = slot.astype(F32)
        live = counts_s[slot].astype(F32)
        sel_row = sel_ref[pl.ds(slot, 1), :].astype(F32)
        limit[o] = turn(sel_row)
        sel_8 = jnp.broadcast_to(sel_row, (8, ROWS)).astype(BF16)
        shift = jnp.where(iota((PAD, ROWS), 0) - KEPT == iota((PAD, ROWS), 1), 1.0, 0.0)
        places = iota((8, TOKENS), 1).astype(BF16)
        diagonal = dot_nt(places, kept_rows(sel_row, live)) + dot_nt(sel_8, shift.astype(BF16))
        diagonal = jnp.broadcast_to(diagonal[:1], (spans, PAD))
        end_kept = jnp.where(slot_of <= at, jnp.minimum(TOKENS - slot_live, float(KEPT)), 0.0)
        end_rows = jnp.where(span_at <= at, KEPT + row_live, 0.0)
        same_kept = jnp.where(slot_of == at, 1.0, 0.0)
        same_rows = jnp.where(span_at == at, 1.0, 0.0)
        is_kept = lane < KEPT
        valid = lane < jnp.where(is_kept, end_kept, end_rows)
        same = jnp.where(is_kept, same_kept, same_rows)
        token_of[o] = jnp.where(valid, same * diagonal, FAR)

    for g in range(GROUP):
        queries[0, g * ROWS:(g + 1) * ROWS, :] = q_ref[
            :, pl.ds(pl.multiple_of(mine_q + g * HEAD, HEAD), HEAD)
        ]
    acc[...] = jnp.zeros_like(acc)
    total[...] = jnp.zeros_like(total)
    top[...] = jnp.full_like(top, LOW)
    blocks[:, :, :, PART:PAD, :] = jnp.zeros((levels, 2, 2, PAD - PART, HEAD), BF16)

    for kv in range(2):
        arrived(0, kv, 1)
        for direction in range(2):
            ring(direction, part(0, kv, 1), 2, kv, direction, kv).start()
    for g in range(GROUP):
        ask(g).wait_recv()

    def absorb(unit):
        distance = (unit + 1) // 2
        half = jnp.where(unit == 0, 0, (unit + 1) % 2)
        column = (y + half) % 2
        whole = (unit == 0) | (unit == last)
        first = ((z + levels - distance) % levels) * 2 + jnp.where(whole, y, column)
        second = ((z + distance) % levels) * 2 + jnp.where(whole, 1 - y, column)
        keys = blocks[unit, 0].reshape(2 * PAD, HEAD)
        values = blocks[unit, 1].reshape(2 * PAD, HEAD)
        values = jnp.concatenate([values, jnp.ones_like(values)], axis=1)
        for o in (1, 0):
            tokens = jnp.concatenate(
                [token_of[o, pl.ds(first, 1), :], token_of[o, pl.ds(second, 1), :]], axis=1
            )
            bound = limit[o]
            seen = jnp.concatenate(
                [tokens[:, j:j + 128] <= bound for j in range(0, 2 * PAD, 128)], axis=1
            )
            for t in range(GROUP * ROWS // TILE):
                rows = slice(t * TILE, (t + 1) * TILE)
                scores = dot_nt(queries[o, rows, :], keys) * SCALE
                scores = scores.reshape(TILE // ROWS, ROWS, 2 * PAD)
                scores = jnp.where(seen[None], scores, LOW).reshape(TILE, 2 * PAD)
                old = top[o, rows, :]
                new = jnp.maximum(old, jnp.max(scores, axis=1, keepdims=True))
                top[o, rows, :] = new
                decay = jnp.exp2(old - new)
                weights = jnp.exp2(scores - jnp.concatenate([new] * (2 * PAD // 128), axis=1))
                found = dot(weights.astype(BF16), values)
                total[o, rows, :] = total[o, rows, :] * decay + found[:, HEAD:]
                acc[o, rows, :] = acc[o, rows, :] * decay + found[:, :HEAD]

    def step(unit, carry):
        @pl.when((unit >= 1) & (unit < last))
        def _():
            for kv in range(2):
                for direction in range(2):
                    arrived(unit, kv, direction)

                    @pl.when(unit < last - 2)
                    def _():
                        ring(
                            direction, part(unit, kv, direction), unit + 2, kv, direction, kv
                        ).start()

                    if kv == direction:
                        @pl.when(unit >= last - 2)
                        def _():
                            half = (unit + 1) % 2
                            ring(
                                direction, part(unit, kv, direction), last, kv, half, half
                            ).start()

        @pl.when(unit == last)
        def _():
            for half in range(2):
                for kv in range(2):
                    arrived(last, kv, half)

        absorb(unit)
        return carry

    lax.fori_loop(0, levels, step, 0)

    def finish(o, g, live):
        rows = slice(g * ROWS, (g + 1) * ROWS)
        result = acc[o, rows, :] / total[o, rows, :]
        return jnp.where(iota((ROWS, HEAD), 0) < live, result, 0.0).astype(BF16)

    def reply(g):
        return send(
            answer.at[g],
            out_ref.at[:, pl.ds(pl.multiple_of(mine_q + g * HEAD, HEAD), HEAD)],
            answer_send.at[g], answer_recv.at[g], {"mirror": partner},
        )

    partner_live = counts_s[partner].astype(F32)
    for g in range(GROUP):
        answer[g] = finish(1, g, partner_live)
        reply(g).start()

    def where_is(slot):
        half = (slot + y) % 2
        ahead = (slot // 2 + levels - z) % levels
        distance = jnp.minimum(ahead, levels - ahead)
        whole = (ahead == 0) | (ahead == half_way)
        unit = jnp.where(ahead == 0, 0, jnp.where(ahead == half_way, last, 2 * distance - 1 + half))
        side = jnp.where(whole, half, jnp.where(ahead < half_way, 1, 0))
        return unit, side

    def find_partner(s, found):
        return jnp.where(order_s[s] == partner, s, found)

    partner_slot = lax.fori_loop(0, spans, find_partner, 0)
    unit, side = where_is(partner_slot)
    for kv in range(2):
        rows_out[kv] = blocks[unit, kv, side, KEPT:PART, :]
    hand = send(rows_out, rows_in, rows_send, rows_recv, {"mirror": partner})
    hand.start()

    own_live = counts_s[me].astype(F32)
    for g in range(GROUP):
        out_ref[:, pl.ds(pl.multiple_of(mine_q + g * HEAD, HEAD), HEAD)] = finish(0, g, own_live)

    unit, side = where_is(my_slot)
    match = (iota((TOKENS, ROWS), 0) == my_sel) & (iota((TOKENS, ROWS), 1) < my_live)
    markers = jnp.where(match, 1.0, 0.0)
    hit = jnp.max(markers, axis=1, keepdims=True)
    markers = markers.astype(BF16)
    side_sel = turn(my_sel)
    side_sel = jnp.concatenate([side_sel, side_sel], axis=1)
    match = (iota((ROWS, TOKENS), 1) == side_sel) & (iota((ROWS, TOKENS), 0) < my_live)
    markers_t = jnp.where(match, 1.0, 0.0).astype(BF16)

    def blend(fresh, cache, result, at):
        moved = dot(markers, fresh)
        old = cache[:, pl.ds(at, HEAD)]
        result[:, pl.ds(at, HEAD)] = jnp.where(hit > 0.5, moved, old.astype(F32)).astype(BF16)

    def gaps(fresh, at):
        gap = fresh.astype(F32) - dot(markers_t, k_ref[:, pl.ds(at, HEAD)])
        return jnp.sum(gap * gap, axis=1, keepdims=True)

    fresh_k = blocks[unit, 0, side, KEPT:PART, :]
    fresh_v = blocks[unit, 1, side, KEPT:PART, :]
    blend(fresh_k, k_ref, mk_ref, mine_at)
    blend(fresh_v, v_ref, mv_ref, mine_at)
    squares = gaps(fresh_k, mine_at)
    hand.wait_recv()
    blend(rows_in[0], k_ref, mk_ref, away_at)
    blend(rows_in[1], v_ref, mv_ref, away_at)
    squares = squares + gaps(rows_in[0], away_at)
    gap_mine[...] = jnp.broadcast_to(squares, (ROWS, ROWS)).T[:8]
    swap = send(gap_mine, gap_other, gap_send, gap_recv, {"tensor": 1 - core})
    swap.start()
    swap.wait_recv()
    mean = (gap_mine[:1] + gap_other[:1]) / (4.0 * HEAD)
    dev_ref[...] = jnp.where(iota((1, ROWS), 1) < my_live, mean, 0.0)

    for g in range(GROUP):
        reply(g).wait_recv()

    swap.wait_send()
    hand.wait_send()
    for g in range(GROUP):
        reply(g).wait_send()
        ask(g).wait_send()
    for kv in range(2):
        across(kv).wait_send()

    def drain(unit, carry):
        for direction in range(2):
            for kv in range(2):
                ring(direction, part(0, 0, 0), unit, kv, 0, kv).wait_send()
        return carry

    lax.fori_loop(1, levels, drain, 0)


def body(k_cache, value_cache, queries, new_keys, new_values, sel_index, counts, span_order):
    spans = sel_index.shape[0]
    levels = spans // 2
    columns = queries.shape[2]
    wide = k_cache.shape[2]
    smem = pl.BlockSpec(memory_space=pltpu.SMEM)
    vmem = pl.BlockSpec(memory_space=pltpu.VMEM)
    dma = pltpu.SemaphoreType.DMA
    stats = pltpu.VMEM((2, GROUP * ROWS, HEAD), F32)
    out, mk, mv, dev = pl.pallas_call(
        functools.partial(kernel, levels),
        out_shape=(
            jax.ShapeDtypeStruct((ROWS, columns), BF16),
            jax.ShapeDtypeStruct((TOKENS, wide), BF16),
            jax.ShapeDtypeStruct((TOKENS, wide), BF16),
            jax.ShapeDtypeStruct((1, ROWS), F32),
        ),
        in_specs=[smem, smem] + [vmem] * 8,
        out_specs=(vmem,) * 4,
        scratch_shapes=[
            pltpu.VMEM((levels, 2, 2, PAD, HEAD), BF16),
            pltpu.VMEM((2, GROUP * ROWS, HEAD), BF16),
            stats,
            stats,
            stats,
            pltpu.VMEM((2, spans, PAD), F32),
            pltpu.VMEM((2, ROWS, ROWS), F32),
            pltpu.VMEM((2, PART, HEAD), BF16),
            pltpu.VMEM((2, ROWS, HEAD), BF16),
            pltpu.VMEM((2, ROWS, HEAD), BF16),
            pltpu.VMEM((GROUP, ROWS, HEAD), BF16),
            pltpu.VMEM((8, ROWS), F32),
            pltpu.VMEM((8, ROWS), F32),
            dma((levels, 2, 2)),
            dma((2, levels, 2)),
            dma((2,)),
            dma((GROUP,)),
            dma((GROUP,)),
            dma,
            dma,
            dma((GROUP,)),
            dma((GROUP,)),
            dma,
            dma,
        ],
        compiler_params=pltpu.CompilerParams(
            collective_id=0, has_side_effects=True, vmem_limit_bytes=48 * 2**20
        ),
    )(
        span_order,
        counts,
        k_cache[0],
        value_cache[0],
        queries[0],
        new_keys[0],
        new_values[0],
        sel_index,
        counts[None],
        span_order[None],
    )
    return out[None], mk[None], mv[None], dev


def solution(mesh):
    whole = P(("request", "mirror"), None, "tensor")
    in_specs = (whole,) * 5 + (P("request", None), P("request"), P("request"))
    out_specs = (whole, whole, whole, P(("request", "mirror"), None))
    return jax.shard_map(body, mesh=mesh, in_specs=in_specs, out_specs=out_specs, check_vma=False)
```

time: 939 us -> 101 us (0.11)
  the two profiles are of different devices: /device:TPU:504 before, /device:TPU:1 now
where the time goes in v1:
time: 101 us
  Pallas kernels  91.3 us (90%)
  local copies, waits for them, and re-layouts  8.51 us (8%)
    pallas_call x1, Pallas kernels, body(): pl.pallas_call(functools.partial(kernel, levels), out_shape=(jax.ShapeDty...  91.3 us
    unnamed x20, local copies, waits for them, and re-layouts  8.51 us

profile of v1, /device:TPU:1, one launch (start us, length us, event | category | flops | bytes accessed | tf_op | source)
XLA Modules:
  0.0 100.5 jit_solution(11492928706453623433)
XLA Ops:
  0.6 0.0 copy-start.6
  0.6 0.0 copy-start.7
  0.7 0.6 copy-done.6
  1.3 0.0 copy-done.7
  1.3 0.0 copy-start
  1.3 1.0 %copy-done = bf16[1,128,2048]{2,1,0:T(8,128)(2,1)S(1)} copy-done((bf16[1,128,2048]{2,1,0:T(8,128)(2,1)S(1)}, bf16[1,128,2048]{2,1,0:T(8,128)(2,1)}, u32[]{:S(2)}) %copy-start) | copy-done | bytes 524312
  2.3 0.0 copy-start.1
  2.4 0.9 copy-done.1
  3.3 0.0 copy-start.2
  3.3 0.9 copy-done.2
  4.2 0.0 copy-start.3
  4.2 0.8 copy-done.3
  5.0 0.0 copy-start.4
  5.0 0.8 copy-done.4
  5.8 0.0 copy-start.5
  5.8 0.7 copy-done.5
  6.6 91.3 %shard_map.111 = (bf16[128,2048]{1,0:T(8,128)(2,1)S(1)}, bf16[256,256]{1,0:T(8,128)(2,1)S(1)}, bf16[256,256]{1,0:T(8,128)(2,1)S(1)}, f32[1,128]{1,0:T(1,128)S(1)}) custom-call(s32[32]{0:T(128)S(1)} %copy-done.6, s32[32]{0:T(128)S(1)} %copy-done.7, bf16[256,256]{1,0:T(8,128)(2,1)S(1)} %bitcast.12, bf16[256,256]{1,0:T(8,128)(2,1)S(1)} %bitcast.13, ...), custom_call_target="tpu_custom_call" | custom-call | tf_op jit(solution)/shard_map/pallas_call | solution.py:388
  97.9 0.8 copy.16
  98.7 0.7 copy.17
  99.4 0.7 copy.18
  100.0 0.5 copy.19
Async XLA Ops:
  0.6 0.7 copy-start.6
  0.6 0.7 copy-start.7
  1.3 1.0 %copy-start = (bf16[1,128,2048]{2,1,0:T(8,128)(2,1)S(1)}, bf16[1,128,2048]{2,1,0:T(8,128)(2,1)}, u32[]{:S(2)}) copy-start(bf16[1,128,2048]{2,1,0:T(8,128)(2,1)} %param.10) | copy-start | bytes 1572868
  2.3 0.9 copy-start.1
  3.3 0.9 copy-start.2
  4.2 0.8 copy-start.3
  5.0 0.8 copy-start.4
  5.8 0.7 copy-start.5

commit v2 on v1

v2 whole, which is shorter than its diff:
```python
import functools
import math

import jax
import jax.numpy as jnp
from jax import lax
from jax.experimental import pallas as pl
from jax.experimental.pallas import tpu as pltpu
from jax.sharding import PartitionSpec as P

HEAD = 128
TOKENS = 256
ROWS = 128
LEAST = 48
KEPT = TOKENS - LEAST
GROUP = 8
TILE = 256
LOW = -1e30
FAR = 1e9
SCALE = math.log2(math.e) / math.sqrt(HEAD)
F32 = jnp.float32
BF16 = jnp.bfloat16


def dot(a, b):
    return jnp.dot(a, b, preferred_element_type=F32)


def dot_nt(a, b):
    return lax.dot_general(a, b, (((1,), (1,)), ((), ())), preferred_element_type=F32)


def iota(shape, dim):
    return lax.broadcasted_iota(jnp.int32, shape, dim).astype(F32)


def turn(row):
    return jnp.broadcast_to(row, (ROWS, ROWS)).T


def kept_rows(sel_row, live):
    places = iota((ROWS, TOKENS), 1)
    side = turn(sel_row)
    side = jnp.concatenate([side, side], axis=1)
    slots = iota((ROWS, TOKENS), 0)
    hits = jnp.where((places == side) & (slots < live), 1.0, 0.0)
    keep = 1.0 - jnp.max(hits, axis=0, keepdims=True)
    before = jnp.where(iota((TOKENS, TOKENS), 0) < iota((TOKENS, TOKENS), 1), 1.0, 0.0)
    rank = dot(jnp.broadcast_to(keep, (8, TOKENS)).astype(BF16), before.astype(BF16))[:1]
    rank = jnp.where(keep > 0.5, rank, -1.0)
    return jnp.where(iota((TOKENS, TOKENS), 0) == rank, 1.0, 0.0).astype(BF16)


def kernel(
    levels,
    order_h,
    counts_h,
    sel_h,
    k_h,
    v_h,
    q_h,
    rk_h,
    rv_h,
    out_ref,
    mk_ref,
    mv_ref,
    dev_ref,
    order_s,
    counts_s,
    order_v,
    counts_v,
    sel_ref,
    k_ref,
    v_ref,
    kept,
    fresh,
    queries,
    acc,
    total,
    top,
    token_kept,
    token_fresh,
    limit,
    away,
    rows_out,
    rows_in,
    answer,
    gap_mine,
    gap_other,
    load_sem,
    query_load,
    block_recv,
    far_recv,
    ring_send,
    far_send,
    away_send,
    query_send,
    query_recv,
    rows_send,
    rows_recv,
    answer_send,
    answer_recv,
    gap_send,
    gap_recv,
):
    spans = 2 * levels
    half_way = levels // 2
    last = levels - 1
    me = lax.axis_index("mirror")
    core = lax.axis_index("tensor")
    z, y = me // 2, me % 2
    partner = z * 2 + 1 - y
    up = ((z + 1) % levels) * 2 + y
    down = ((z + levels - 1) % levels) * 2 + y
    mine_at = pl.multiple_of(y * HEAD, HEAD)
    away_at = pl.multiple_of((1 - y) * HEAD, HEAD)
    mine_q = y * GROUP * HEAD
    away_q = (1 - y) * GROUP * HEAD

    barrier = pltpu.get_barrier_semaphore()
    for other in (up, down, partner):
        pl.semaphore_signal(barrier, inc=1, device_id={"mirror": other})
    pl.semaphore_signal(barrier, inc=1, device_id={"tensor": 1 - core})

    def q_columns(at, g):
        return q_h.at[:, pl.ds(pl.multiple_of(at + g * HEAD, HEAD), HEAD)]

    loads = [
        pltpu.make_async_copy(src, dst, load_sem.at[i])
        for i, (src, dst) in enumerate(
            (
                (order_h, order_s),
                (counts_h, counts_s),
                (order_h, order_v),
                (counts_h, counts_v),
                (sel_h, sel_ref),
                (k_h, k_ref),
                (v_h, v_ref),
                (rk_h.at[:, pl.ds(mine_at, HEAD)], fresh.at[0, 0, 0]),
                (rv_h.at[:, pl.ds(mine_at, HEAD)], fresh.at[0, 1, 0]),
            )
        )
    ]
    for load in loads:
        load.start()

    def load_query(g):
        return pltpu.make_async_copy(
            q_columns(mine_q, g), queries.at[0, pl.ds(g * ROWS, ROWS), :], query_load.at[g]
        )

    for g in range(GROUP):
        load_query(g).start()

    def send(src, dst, send_sem, recv_sem, to):
        return pltpu.make_async_remote_copy(
            src_ref=src, dst_ref=dst, send_sem=send_sem, recv_sem=recv_sem, device_id=to
        )

    def rows_of(unit, slot):
        return fresh.at[unit, :, slot]

    def kept_of(unit, slot):
        return kept.at[unit, :, slot, pl.ds(0, KEPT), :]

    def way(direction):
        return {"mirror": up if direction == 0 else down}

    def ring(direction, unit, slot, kind, to_unit):
        piece = (rows_of, kept_of)[kind]
        return send(
            piece(unit, slot), piece(to_unit, direction), ring_send.at[direction, to_unit, kind],
            block_recv.at[to_unit, direction, kind], way(direction),
        )

    def far(kv, half, kind, unit):
        if kind == 0:
            src, dst = fresh.at[unit, kv, kv], fresh.at[last, kv, half]
        else:
            src = kept.at[unit, kv, kv, pl.ds(0, KEPT), :]
            dst = kept.at[last, kv, half, pl.ds(0, KEPT), :]
        return send(src, dst, far_send.at[kv, half, kind], far_recv.at[kv, half, kind], way(kv))

    def arrived(unit, slot, kind):
        piece = (rows_of, kept_of)[kind]
        send(
            piece(unit, slot), piece(unit, slot), ring_send.at[0, 0, 0],
            block_recv.at[unit, slot, kind], way(0),
        ).wait_recv()

    acc[...] = jnp.zeros_like(acc)
    total[...] = jnp.zeros_like(total)
    top[...] = jnp.full_like(top, LOW)
    kept[:, 1, :, KEPT:, :] = jnp.zeros((levels, 2, TOKENS - KEPT, HEAD), BF16)

    pl.semaphore_wait(barrier, 4)

    for kv, rows_h in enumerate((rk_h, rv_h)):
        send(
            rows_h.at[:, pl.ds(away_at, HEAD)], fresh.at[0, kv, 1], away_send.at[0],
            block_recv.at[0, 1, 0], {"mirror": partner},
        ).start()
        for direction in range(2):
            send(
                rows_h.at[:, pl.ds(mine_at, HEAD)], fresh.at[1, kv, direction],
                ring_send.at[direction, 1, 0], block_recv.at[1, direction, 0], way(direction),
            ).start()

    for load in loads:
        load.wait()

    def find(s, found):
        return jnp.where(order_s[0, s] == me, s, found)

    my_slot = lax.fori_loop(0, spans, find, 0)
    my_live = counts_s[0, my_slot].astype(F32)
    sel_all = sel_ref[...].astype(F32)
    chosen = jnp.where(order_v[...] == me, 1.0, 0.0)
    my_sel = dot(jnp.broadcast_to(chosen, (8, spans)).astype(BF16), sel_all.astype(BF16))[:1]

    keep_mine = kept_rows(my_sel, my_live)[:KEPT]
    for kv, cache in enumerate((k_ref, v_ref)):
        away[kv] = dot(keep_mine, cache[:, pl.ds(away_at, HEAD)]).astype(BF16)
    across = send(
        away, kept_of(0, 1), away_send.at[1], block_recv.at[0, 1, 1], {"mirror": partner}
    )
    across.start()
    for kv, cache in enumerate((k_ref, v_ref)):
        kept[0, kv, 0, 0:KEPT, :] = dot(keep_mine, cache[:, pl.ds(mine_at, HEAD)]).astype(BF16)
    for direction in range(2):
        ring(direction, 0, 0, 1, 1).start()

    def ask(g):
        return send(
            q_columns(away_q, g), queries.at[1, pl.ds(g * ROWS, ROWS), :],
            query_send.at[g], query_recv.at[g], {"mirror": partner},
        )

    for g in range(GROUP):
        ask(g).start()

    arrived(0, 1, 0)
    for direction in range(2):
        ring(direction, 0, 1, 0, 2).start()

    counts_f = counts_v[...].astype(F32)
    c_at, s_at = iota((spans, spans), 0), iota((spans, spans), 1)
    pick = order_v[...].astype(F32) == c_at
    slot_of = jnp.sum(jnp.where(pick, s_at, 0.0), axis=1, keepdims=True)
    slot_live = jnp.sum(jnp.where(pick, counts_f, 0.0), axis=1, keepdims=True)
    row_live = jnp.sum(jnp.where(c_at == s_at, counts_f, 0.0), axis=1, keepdims=True)
    span_at = iota((spans, ROWS), 0)[:, :1]
    for o, slot in ((0, me), (1, partner)):
        at = slot.astype(F32)
        live = counts_s[0, slot].astype(F32)
        sel_row = sel_ref[pl.ds(slot, 1), :].astype(F32)
        limit[o] = turn(sel_row)
        places = iota((8, TOKENS), 1).astype(BF16)
        diagonal = dot_nt(places, kept_rows(sel_row, live))[:1]
        end = jnp.where(slot_of <= at, jnp.minimum(TOKENS - slot_live, float(KEPT)), 0.0)
        same = jnp.where(slot_of == at, 1.0, 0.0)
        token_kept[o] = jnp.where(iota((spans, TOKENS), 1) < end, same * diagonal, FAR)
        end = jnp.where(span_at <= at, row_live, 0.0)
        same = jnp.where(span_at == at, 1.0, 0.0)
        token_fresh[o] = jnp.where(iota((spans, ROWS), 1) < end, same * sel_row, FAR)

    arrived(0, 1, 1)
    for direction in range(2):
        ring(direction, 0, 1, 1, 2).start()
    for g in range(GROUP):
        load_query(g).wait()
        ask(g).wait_recv()

    def attend(o, spans_at, keys, values, after=None):
        tokens = jnp.concatenate(
            [token_kept[o, pl.ds(c, 1), :] for c in spans_at]
            + [token_fresh[o, pl.ds(c, 1), :] for c in spans_at],
            axis=1,
        )
        wide = tokens.shape[1]
        split = keys[0].shape[0]
        bound = limit[o]
        seen = jnp.concatenate(
            [tokens[:, j:j + HEAD] <= bound for j in range(0, wide, HEAD)], axis=1
        )
        values = [jnp.concatenate([v, jnp.ones_like(v)], axis=1) for v in values]
        for t in range(GROUP * ROWS // TILE):
            rows = slice(t * TILE, (t + 1) * TILE)
            q = queries[o, rows, :]
            scores = jnp.concatenate([dot_nt(q, k) for k in keys], axis=1) * SCALE
            scores = scores.reshape(TILE // ROWS, ROWS, wide)
            scores = jnp.where(seen[None], scores, LOW).reshape(TILE, wide)
            old = top[o, rows, :]
            new = jnp.maximum(old, jnp.max(scores, axis=1, keepdims=True))
            decay = jnp.exp2(old - new)
            weights = jnp.exp2(scores - jnp.concatenate([new] * (wide // HEAD), axis=1))
            weights = weights.astype(BF16)
            found = dot(weights[:, :split], values[0]) + dot(weights[:, split:], values[1])
            sums = total[o, rows, :] * decay + found[:, HEAD:]
            mixed = acc[o, rows, :] * decay + found[:, :HEAD]
            if after is not None:
                after(t, mixed / sums)
            else:
                top[o, rows, :] = new
                total[o, rows, :] = sums
                acc[o, rows, :] = mixed

    def absorb(unit, o):
        distance = (unit + 1) // 2
        half = jnp.where(unit == 0, 0, (unit + 1) % 2)
        column = (y + half) % 2
        whole = (unit == 0) | (unit == last)
        first = ((z + levels - distance) % levels) * 2 + jnp.where(whole, y, column)
        second = ((z + distance) % levels) * 2 + jnp.where(whole, 1 - y, column)
        both = [
            (kept[unit, kv].reshape(2 * TOKENS, HEAD), fresh[unit, kv].reshape(2 * ROWS, HEAD))
            for kv in range(2)
        ]
        attend(o, (first, second), *both)

    def relay(unit):
        for kind in range(2):
            for direction in range(2):
                arrived(unit, direction, kind)

                @pl.when(unit < last - 2)
                def _():
                    ring(direction, unit, direction, kind, unit + 2).start()

                @pl.when(unit >= last - 2)
                def _():
                    far(direction, (unit + 1) % 2, kind, unit).start()

    def step(unit, carry):
        @pl.when(unit > 0)
        def _():
            relay(unit)

        for o in (1, 0):
            absorb(unit, o)
        return carry

    lax.fori_loop(0, last - 1, step, 0)
    relay(last - 1)
    absorb(last - 1, 1)

    def reply(g):
        return send(
            answer.at[g],
            out_ref.at[:, pl.ds(pl.multiple_of(mine_q + g * HEAD, HEAD), HEAD)],
            answer_send.at[g], answer_recv.at[g], {"mirror": partner},
        )

    def far_half(half, after=None):
        attend(
            1,
            (((z + half_way) % levels) * 2 + (y + half) % 2,),
            *[(kept[last, kv, half], fresh[last, kv, half]) for kv in range(2)],
            after=after,
        )

    def far_arrived(half, kind):
        for kv in range(2):
            far(kv, half, kind, last).wait_recv()

    far_arrived(0, 0)
    far_arrived(0, 1)
    far_half(0)
    far_arrived(1, 0)

    def where_is(slot):
        half = (slot + y) % 2
        ahead = (slot // 2 + levels - z) % levels
        distance = jnp.minimum(ahead, levels - ahead)
        whole = (ahead == 0) | (ahead == half_way)
        unit = jnp.where(ahead == 0, 0, jnp.where(ahead == half_way, last, 2 * distance - 1 + half))
        side = jnp.where(whole, half, jnp.where(ahead < half_way, 1, 0))
        return unit, side

    def find_partner(s, found):
        return jnp.where(order_s[0, s] == partner, s, found)

    partner_slot = lax.fori_loop(0, spans, find_partner, 0)
    unit, side = where_is(partner_slot)
    for kv in range(2):
        rows_out[kv] = fresh[unit, kv, side]
    hand = send(rows_out, rows_in, rows_send, rows_recv, {"mirror": partner})
    hand.start()

    far_arrived(1, 1)
    partner_live = counts_s[0, partner].astype(F32)
    own_live = counts_s[0, me].astype(F32)

    def live_only(result, live):
        return jnp.where(iota((ROWS, HEAD), 0) < live, result, 0.0).astype(BF16)

    def give_back(t, result):
        for i in range(TILE // ROWS):
            g = t * (TILE // ROWS) + i
            answer[g] = live_only(result[i * ROWS:(i + 1) * ROWS], partner_live)
            reply(g).start()

    far_half(1, give_back)

    unit, side = where_is(my_slot)
    match = (iota((TOKENS, ROWS), 0) == my_sel) & (iota((TOKENS, ROWS), 1) < my_live)
    markers = jnp.where(match, 1.0, 0.0)
    hit = jnp.max(markers, axis=1, keepdims=True)
    markers = markers.astype(BF16)
    side_sel = turn(my_sel)
    side_sel = jnp.concatenate([side_sel, side_sel], axis=1)
    match = (iota((ROWS, TOKENS), 1) == side_sel) & (iota((ROWS, TOKENS), 0) < my_live)
    markers_t = jnp.where(match, 1.0, 0.0).astype(BF16)

    def blend(new_rows, cache, result, at):
        moved = dot(markers, new_rows)
        old = cache[:, pl.ds(at, HEAD)]
        result[:, pl.ds(at, HEAD)] = jnp.where(hit > 0.5, moved, old.astype(F32)).astype(BF16)

    def gaps(new_rows, at):
        gap = new_rows.astype(F32) - dot(markers_t, k_ref[:, pl.ds(at, HEAD)])
        return jnp.sum(gap * gap, axis=1, keepdims=True)

    fresh_k = fresh[unit, 0, side]
    fresh_v = fresh[unit, 1, side]
    hand.wait_recv()
    squares = gaps(fresh_k, mine_at) + gaps(rows_in[0], away_at)
    gap_mine[...] = jnp.broadcast_to(squares, (ROWS, ROWS)).T[:8]
    swap = send(gap_mine, gap_other, gap_send, gap_recv, {"tensor": 1 - core})
    swap.start()
    blend(fresh_k, k_ref, mk_ref, mine_at)
    blend(fresh_v, v_ref, mv_ref, mine_at)
    blend(rows_in[0], k_ref, mk_ref, away_at)
    blend(rows_in[1], v_ref, mv_ref, away_at)

    def own_rest(unit, carry):
        absorb(unit, 0)
        return carry

    lax.fori_loop(last - 1, levels, own_rest, 0)
    for g in range(GROUP):
        rows = slice(g * ROWS, (g + 1) * ROWS)
        out_ref[:, pl.ds(pl.multiple_of(mine_q + g * HEAD, HEAD), HEAD)] = live_only(
            acc[0, rows, :] / total[0, rows, :], own_live
        )
    swap.wait_recv()
    mean = (gap_mine[:1] + gap_other[:1]) / (4.0 * HEAD)
    dev_ref[...] = jnp.where(iota((1, ROWS), 1) < my_live, mean, 0.0)

    swap.wait_send()
    hand.wait_send()
    across.wait_send()
    send(
        rows_of(0, 1), rows_of(0, 1), away_send.at[0], block_recv.at[0, 1, 0], way(0)
    ).wait_send()
    for kv in range(2):
        for half in range(2):
            for kind in range(2):
                far(kv, half, kind, last).wait_send()

    def drain(unit, carry):
        for direction in range(2):
            for kind in range(2):
                ring(direction, unit, direction, kind, unit).wait_send()
        return carry

    lax.fori_loop(1, last, drain, 0)
    for g in range(GROUP):
        ask(g).wait_send()
    for g in range(GROUP):
        reply(g).wait_recv()
        reply(g).wait_send()


def deliver(*refs):
    count = (len(refs) - 1) // 2
    sems = refs[-1]
    copies = [
        pltpu.make_async_copy(refs[i], refs[count + i], sems.at[i]) for i in range(count)
    ]
    for copy in copies:
        copy.start()
    for copy in copies:
        copy.wait()


def body(k_cache, value_cache, queries, new_keys, new_values, sel_index, counts, span_order):
    spans = sel_index.shape[0]
    levels = spans // 2
    columns = queries.shape[2]
    wide = k_cache.shape[2]
    hbm = pl.BlockSpec(memory_space=pltpu.HBM)
    vmem = pl.BlockSpec(memory_space=pltpu.VMEM)
    dma = pltpu.SemaphoreType.DMA
    stats = pltpu.VMEM((2, GROUP * ROWS, HEAD), F32)
    shapes = (
        jax.ShapeDtypeStruct((ROWS, columns), BF16),
        jax.ShapeDtypeStruct((TOKENS, wide), BF16),
        jax.ShapeDtypeStruct((TOKENS, wide), BF16),
        jax.ShapeDtypeStruct((1, ROWS), F32),
    )
    results = pl.pallas_call(
        functools.partial(kernel, levels),
        out_shape=shapes,
        in_specs=[hbm] * 8,
        out_specs=(vmem,) * 4,
        scratch_shapes=[
            pltpu.SMEM((1, spans), jnp.int32),
            pltpu.SMEM((1, spans), jnp.int32),
            pltpu.VMEM((1, spans), jnp.int32),
            pltpu.VMEM((1, spans), jnp.int32),
            pltpu.VMEM((spans, ROWS), jnp.int32),
            pltpu.VMEM((TOKENS, wide), BF16),
            pltpu.VMEM((TOKENS, wide), BF16),
            pltpu.VMEM((levels, 2, 2, TOKENS, HEAD), BF16),
            pltpu.VMEM((levels, 2, 2, ROWS, HEAD), BF16),
            pltpu.VMEM((2, GROUP * ROWS, HEAD), BF16),
            stats,
            stats,
            stats,
            pltpu.VMEM((2, spans, TOKENS), F32),
            pltpu.VMEM((2, spans, ROWS), F32),
            pltpu.VMEM((2, ROWS, ROWS), F32),
            pltpu.VMEM((2, KEPT, HEAD), BF16),
            pltpu.VMEM((2, ROWS, HEAD), BF16),
            pltpu.VMEM((2, ROWS, HEAD), BF16),
            pltpu.VMEM((GROUP, ROWS, HEAD), BF16),
            pltpu.VMEM((8, ROWS), F32),
            pltpu.VMEM((8, ROWS), F32),
            dma((9,)),
            dma((GROUP,)),
            dma((levels, 2, 2)),
            dma((2, 2, 2)),
            dma((2, levels, 2)),
            dma((2, 2, 2)),
            dma((2,)),
            dma((GROUP,)),
            dma((GROUP,)),
            dma,
            dma,
            dma((GROUP,)),
            dma((GROUP,)),
            dma,
            dma,
        ],
        compiler_params=pltpu.CompilerParams(
            collective_id=0, has_side_effects=True, vmem_limit_bytes=48 * 2**20
        ),
    )(
        span_order[None],
        counts[None],
        sel_index,
        k_cache[0],
        value_cache[0],
        queries[0],
        new_keys[0],
        new_values[0],
    )
    out, mk, mv, dev = pl.pallas_call(
        deliver,
        out_shape=shapes,
        in_specs=[vmem] * 4,
        out_specs=(hbm,) * 4,
        scratch_shapes=[dma((4,))],
    )(*results)
    return out[None], mk[None], mv[None], dev


def solution(mesh):
    whole = P(("request", "mirror"), None, "tensor")
    in_specs = (whole,) * 5 + (P("request", None), P("request"), P("request"))
    out_specs = (whole, whole, whole, P(("request", "mirror"), None))
    return jax.shard_map(body, mesh=mesh, in_specs=in_specs, out_specs=out_specs, check_vma=False)
```

time: 101 us -> 98.3 us (0.973); the launches traced: 101 us -> 96.8 us
  Pallas kernels: 91.3 us -> 87.6 us
    pallas_call x1 -> x2, Pallas kernels: 91.3 us -> 87.6 us  [the longest x1 85.6 us: body(): pl.pallas_call(functools.partial(kernel, levels), out_shape=shapes, in_sp...]
    unnamed x20 -> x24, local copies, waits for them, and re-layouts: 8.51 us -> 8.49 us
where the time goes in v2:
time: 98.3 us; the launch traced here: 96.8 us
  Pallas kernels  87.6 us (89%)
  local copies, waits for them, and re-layouts  8.49 us (9%)
    pallas_call x1, Pallas kernels, body(): pl.pallas_call(functools.partial(kernel, levels), out_shape=shapes, in_sp...  85.6 us
    unnamed x24, local copies, waits for them, and re-layouts  8.49 us
    pallas_call x1, Pallas kernels, body(): pl.pallas_call(deliver, out_shape=shapes, in_specs=[vmem] * 4, out_specs=...  2.04 us

profile of v2, /device:TPU:1, one launch (start us, length us, event | category | flops | bytes accessed | tf_op | source)
XLA Modules:
  0.0 96.8 jit_solution(13925115460827540628)
XLA Ops:
  0.6 0.0 copy-start.9
  0.6 0.0 copy-start.10
  0.7 0.6 copy-done.9
  1.3 0.0 copy-done.10
  1.3 0.0 copy-start
  1.3 1.0 %copy-done = bf16[1,128,2048]{2,1,0:T(8,128)(2,1)S(1)} copy-done((bf16[1,128,2048]{2,1,0:T(8,128)(2,1)S(1)}, bf16[1,128,2048]{2,1,0:T(8,128)(2,1)}, u32[]{:S(2)}) %copy-start) | copy-done | bytes 524312
  2.3 0.0 copy-start.2
  2.4 0.9 copy-done.2
  3.3 0.0 copy-start.3
  3.3 0.9 copy-done.3
  4.2 0.0 copy-start.6
  4.2 0.8 copy-done.6
  5.0 0.0 copy-start.7
  5.0 0.8 copy-done.7
  5.8 0.0 copy-start.8
  5.8 0.7 copy-done.8
  6.6 85.6 %shard_map.111 = (bf16[128,2048]{1,0:T(8,128)(2,1)S(1)}, bf16[256,256]{1,0:T(8,128)(2,1)S(1)}, bf16[256,256]{1,0:T(8,128)(2,1)S(1)}, f32[1,128]{1,0:T(1,128)S(1)}) custom-call(s32[1,32]{1,0:T(1,128)S(1)} %bitcast.15, s32[1,32]{1,0:T(1,128)S(1)} %bitcast.16, s32[32,128]{1,0:T(8,128)S(1)} %copy-done.8, bf16[256,256]{1,0:T(8,128)(2,1)S(1)} %bitcast.11, ...), custom_call_target="tpu_custom_call" | custom-call | tf_op jit(solution)/shard_map/pallas_call | solution.py:502
  92.2 0.0 copy-start.1
  92.2 0.8 copy-done.1
  93.0 0.0 copy-start.4
  93.0 0.6 copy-done.4
  93.6 0.0 copy-start.5
  93.6 0.7 copy-done.5
  94.3 0.0 copy-start.11
  94.3 0.5 copy-done.11
  94.8 2.0 %shard_map.112 = (bf16[128,2048]{1,0:T(8,128)(2,1)}, bf16[256,256]{1,0:T(8,128)(2,1)}, bf16[256,256]{1,0:T(8,128)(2,1)}, f32[1,128]{1,0:T(1,128)}) custom-call(bf16[128,2048]{1,0:T(8,128)(2,1)} %copy-done.1, bf16[256,256]{1,0:T(8,128)(2,1)} %copy-done.4, bf16[256,256]{1,0:T(8,128)(2,1)} %copy-done.5, f32[1,128]{1,0:T(1,128)} %copy-done.11), custom_call_target="tpu_custom_call" | custom-call | tf_op jit(solution)/shard_map/pallas_call | solution.py:559
Async XLA Ops:
  0.6 0.7 copy-start.9
  0.6 0.7 copy-start.10
  1.3 1.0 %copy-start = (bf16[1,128,2048]{2,1,0:T(8,128)(2,1)S(1)}, bf16[1,128,2048]{2,1,0:T(8,128)(2,1)}, u32[]{:S(2)}) copy-start(bf16[1,128,2048]{2,1,0:T(8,128)(2,1)} %param.10) | copy-start | bytes 1572868
  2.3 0.9 copy-start.2
  3.3 0.9 copy-start.3
  4.2 0.8 copy-start.6
  5.0 0.8 copy-start.7
  5.8 0.7 copy-start.8
  92.2 0.8 copy-start.1
  93.0 0.6 copy-start.4
  93.6 0.7 copy-start.5
  94.3 0.5 copy-start.11

commit v3 on v2

--- a/solution.py
+++ b/solution.py
@@ -14,6 +14,7 @@
 LEAST = 48
 KEPT = TOKENS - LEAST
 GROUP = 8
+VMEM_BYTES = 64 * 2**20 - 2**17
 TILE = 256
 LOW = -1e30
 FAR = 1e9
@@ -61,7 +62,10 @@
     q_h,
     rk_h,
     rv_h,
-    out_ref,
+    out_h,
+    mk_h,
+    mv_h,
+    dev_h,
     mk_ref,
     mv_ref,
     dev_ref,
@@ -85,9 +89,12 @@
     rows_out,
     rows_in,
     answer,
+    own_out,
     gap_mine,
     gap_other,
     load_sem,
+    store_sem,
+    own_sem,
     query_load,
     block_recv,
     far_recv,
@@ -125,32 +132,29 @@
     def q_columns(at, g):
         return q_h.at[:, pl.ds(pl.multiple_of(at + g * HEAD, HEAD), HEAD)]
 
+    def load(src, dst, i):
+        return pltpu.make_async_copy(src, dst, load_sem.at[i])
+
     loads = [
-        pltpu.make_async_copy(src, dst, load_sem.at[i])
-        for i, (src, dst) in enumerate(
-            (
-                (order_h, order_s),
-                (counts_h, counts_s),
-                (order_h, order_v),
-                (counts_h, counts_v),
-                (sel_h, sel_ref),
-                (k_h, k_ref),
-                (v_h, v_ref),
-                (rk_h.at[:, pl.ds(mine_at, HEAD)], fresh.at[0, 0, 0]),
-                (rv_h.at[:, pl.ds(mine_at, HEAD)], fresh.at[0, 1, 0]),
-            )
-        )
+        load(sel_h, sel_ref, 0),
+        load(order_h, order_v, 1),
+        load(counts_h, counts_v, 2),
+        load(k_h, k_ref, 3),
+        load(v_h, v_ref, 4),
     ]
-    for load in loads:
-        load.start()
+    later = [
+        load(order_h, order_s, 5),
+        load(counts_h, counts_s, 6),
+        load(rk_h.at[:, pl.ds(mine_at, HEAD)], fresh.at[0, 0, 0], 7),
+        load(rv_h.at[:, pl.ds(mine_at, HEAD)], fresh.at[0, 1, 0], 8),
+    ]
+    for copy in loads:
+        copy.start()
 
     def load_query(g):
         return pltpu.make_async_copy(
             q_columns(mine_q, g), queries.at[0, pl.ds(g * ROWS, ROWS), :], query_load.at[g]
         )
-
-    for g in range(GROUP):
-        load_query(g).start()
 
     def send(src, dst, send_sem, recv_sem, to):
         return pltpu.make_async_remote_copy(
@@ -188,35 +192,27 @@
             block_recv.at[unit, slot, kind], way(0),
         ).wait_recv()
 
-    acc[...] = jnp.zeros_like(acc)
-    total[...] = jnp.zeros_like(total)
-    top[...] = jnp.full_like(top, LOW)
-    kept[:, 1, :, KEPT:, :] = jnp.zeros((levels, 2, TOKENS - KEPT, HEAD), BF16)
-
     pl.semaphore_wait(barrier, 4)
 
     for kv, rows_h in enumerate((rk_h, rv_h)):
-        send(
-            rows_h.at[:, pl.ds(away_at, HEAD)], fresh.at[0, kv, 1], away_send.at[0],
-            block_recv.at[0, 1, 0], {"mirror": partner},
-        ).start()
         for direction in range(2):
             send(
                 rows_h.at[:, pl.ds(mine_at, HEAD)], fresh.at[1, kv, direction],
                 ring_send.at[direction, 1, 0], block_recv.at[1, direction, 0], way(direction),
             ).start()
-
-    for load in loads:
-        load.wait()
-
-    def find(s, found):
-        return jnp.where(order_s[0, s] == me, s, found)
-
-    my_slot = lax.fori_loop(0, spans, find, 0)
-    my_live = counts_s[0, my_slot].astype(F32)
+        send(
+            rows_h.at[:, pl.ds(away_at, HEAD)], fresh.at[0, kv, 1], away_send.at[0],
+            block_recv.at[0, 1, 0], {"mirror": partner},
+        ).start()
+    for copy in loads:
+        copy.wait()
+    for copy in later:
+        copy.start()
+
     sel_all = sel_ref[...].astype(F32)
     chosen = jnp.where(order_v[...] == me, 1.0, 0.0)
     my_sel = dot(jnp.broadcast_to(chosen, (8, spans)).astype(BF16), sel_all.astype(BF16))[:1]
+    my_live = jnp.sum(chosen * counts_v[...].astype(F32), axis=1, keepdims=True)
 
     keep_mine = kept_rows(my_sel, my_live)[:KEPT]
     for kv, cache in enumerate((k_ref, v_ref)):
@@ -237,11 +233,16 @@
         )
 
     for g in range(GROUP):
-        ask(g).start()
-
+        load_query(g).start()
+    for copy in later:
+        copy.wait()
     arrived(0, 1, 0)
     for direction in range(2):
         ring(direction, 0, 1, 0, 2).start()
+    acc[...] = jnp.zeros_like(acc)
+    total[...] = jnp.zeros_like(total)
+    top[...] = jnp.full_like(top, LOW)
+    kept[:, 1, :, KEPT:, :] = jnp.zeros((levels, 2, TOKENS - KEPT, HEAD), BF16)
 
     counts_f = counts_v[...].astype(F32)
     c_at, s_at = iota((spans, spans), 0), iota((spans, spans), 1)
@@ -264,12 +265,14 @@
         same = jnp.where(span_at == at, 1.0, 0.0)
         token_fresh[o] = jnp.where(iota((spans, ROWS), 1) < end, same * sel_row, FAR)
 
+    across.wait_send()
+    for g in range(GROUP):
+        ask(g).start()
     arrived(0, 1, 1)
     for direction in range(2):
         ring(direction, 0, 1, 1, 2).start()
     for g in range(GROUP):
         load_query(g).wait()
-        ask(g).wait_recv()
 
     def attend(o, spans_at, keys, values, after=None):
         tokens = jnp.concatenate(
@@ -331,23 +334,52 @@
                 def _():
                     far(direction, (unit + 1) % 2, kind, unit).start()
 
+    def find(s, found):
+        return tuple(
+            jnp.where(order_s[0, s] == span, s, slot) for span, slot in zip((me, partner), found)
+        )
+
+    my_slot, partner_slot = lax.fori_loop(0, spans, find, (0, 0))
+
+    def early(i, carry):
+        for at, unit in ((0, 1), (1, 2), (3, 3)):
+            @pl.when(i == at)
+            def _():
+                relay(unit)
+
+        @pl.when(i == 2)
+        def _():
+            for g in range(GROUP):
+                ask(g).wait_recv()
+
+        o = jnp.where((i >= 2) & (i <= 4), 1, 0)
+        absorb(jnp.where(i < 2, i, jnp.where(i < 5, i - 2, 2)), o)
+        return carry
+
+    lax.fori_loop(0, 6, early, 0)
+
     def step(unit, carry):
-        @pl.when(unit > 0)
-        def _():
-            relay(unit)
-
+        relay(unit)
         for o in (1, 0):
-            absorb(unit, o)
+            absorb(unit - 1, o)
         return carry
 
-    lax.fori_loop(0, last - 1, step, 0)
+    lax.fori_loop(4, last - 1, step, 0)
     relay(last - 1)
-    absorb(last - 1, 1)
+
+    def late(unit, carry):
+        absorb(unit, 1)
+        return carry
+
+    lax.fori_loop(last - 2, last, late, 0)
+
+    def out_columns(g):
+        return out_h.at[:, pl.ds(pl.multiple_of(mine_q + g * HEAD, HEAD), HEAD)]
 
     def reply(g):
         return send(
             answer.at[g],
-            out_ref.at[:, pl.ds(pl.multiple_of(mine_q + g * HEAD, HEAD), HEAD)],
+            out_columns(g),
             answer_send.at[g], answer_recv.at[g], {"mirror": partner},
         )
 
@@ -377,10 +409,6 @@
         side = jnp.where(whole, half, jnp.where(ahead < half_way, 1, 0))
         return unit, side
 
-    def find_partner(s, found):
-        return jnp.where(order_s[0, s] == partner, s, found)
-
-    partner_slot = lax.fori_loop(0, spans, find_partner, 0)
     unit, side = where_is(partner_slot)
     for kv in range(2):
         rows_out[kv] = fresh[unit, kv, side]
@@ -433,23 +461,33 @@
     blend(rows_in[0], k_ref, mk_ref, away_at)
     blend(rows_in[1], v_ref, mv_ref, away_at)
 
+    stores = [
+        pltpu.make_async_copy(mk_ref, mk_h, store_sem.at[0]),
+        pltpu.make_async_copy(mv_ref, mv_h, store_sem.at[1]),
+    ]
+    for store in stores:
+        store.start()
+
     def own_rest(unit, carry):
         absorb(unit, 0)
         return carry
 
-    lax.fori_loop(last - 1, levels, own_rest, 0)
+    lax.fori_loop(last - 2, levels, own_rest, 0)
+    def keep(g):
+        return pltpu.make_async_copy(own_out.at[g], out_columns(g), own_sem.at[g])
+
     for g in range(GROUP):
         rows = slice(g * ROWS, (g + 1) * ROWS)
-        out_ref[:, pl.ds(pl.multiple_of(mine_q + g * HEAD, HEAD), HEAD)] = live_only(
-            acc[0, rows, :] / total[0, rows, :], own_live
-        )
+        own_out[g] = live_only(acc[0, rows, :] / total[0, rows, :], own_live)
+        keep(g).start()
     swap.wait_recv()
     mean = (gap_mine[:1] + gap_other[:1]) / (4.0 * HEAD)
     dev_ref[...] = jnp.where(iota((1, ROWS), 1) < my_live, mean, 0.0)
+    store_dev = pltpu.make_async_copy(dev_ref, dev_h, store_sem.at[2])
+    store_dev.start()
 
     swap.wait_send()
     hand.wait_send()
-    across.wait_send()
     send(
         rows_of(0, 1), rows_of(0, 1), away_send.at[0], block_recv.at[0, 1, 0], way(0)
     ).wait_send()
@@ -467,21 +505,29 @@
     lax.fori_loop(1, last, drain, 0)
     for g in range(GROUP):
         ask(g).wait_send()
+    for store in stores + [store_dev] + [keep(g) for g in range(GROUP)]:
+        store.wait()
     for g in range(GROUP):
         reply(g).wait_recv()
         reply(g).wait_send()
 
 
 def deliver(*refs):
-    count = (len(refs) - 1) // 2
-    sems = refs[-1]
-    copies = [
-        pltpu.make_async_copy(refs[i], refs[count + i], sems.at[i]) for i in range(count)
+    count = (len(refs) - 2) // 3
+    held, sems_in, sems_out = refs[2 * count:3 * count], refs[-2], refs[-1]
+    takes = [
+        pltpu.make_async_copy(refs[i], held[i], sems_in.at[i]) for i in range(count)
     ]
-    for copy in copies:
-        copy.start()
-    for copy in copies:
-        copy.wait()
+    gives = [
+        pltpu.make_async_copy(held[i], refs[count + i], sems_out.at[i]) for i in range(count)
+    ]
+    for take in takes:
+        take.start()
+    for take, give in zip(takes, gives):
+        take.wait()
+        give.start()
+    for give in gives:
+        give.wait()
 
 
 def body(k_cache, value_cache, queries, new_keys, new_values, sel_index, counts, span_order):
@@ -490,7 +536,6 @@
     columns = queries.shape[2]
     wide = k_cache.shape[2]
     hbm = pl.BlockSpec(memory_space=pltpu.HBM)
-    vmem = pl.BlockSpec(memory_space=pltpu.VMEM)
     dma = pltpu.SemaphoreType.DMA
     stats = pltpu.VMEM((2, GROUP * ROWS, HEAD), F32)
     shapes = (
@@ -503,8 +548,11 @@
         functools.partial(kernel, levels),
         out_shape=shapes,
         in_specs=[hbm] * 8,
-        out_specs=(vmem,) * 4,
+        out_specs=(hbm,) * 4,
         scratch_shapes=[
+            pltpu.VMEM((TOKENS, wide), BF16),
+            pltpu.VMEM((TOKENS, wide), BF16),
+            pltpu.VMEM((1, ROWS), F32),
             pltpu.SMEM((1, spans), jnp.int32),
             pltpu.SMEM((1, spans), jnp.int32),
             pltpu.VMEM((1, spans), jnp.int32),
@@ -525,9 +573,12 @@
             pltpu.VMEM((2, ROWS, HEAD), BF16),
             pltpu.VMEM((2, ROWS, HEAD), BF16),
             pltpu.VMEM((GROUP, ROWS, HEAD), BF16),
+            pltpu.VMEM((GROUP, ROWS, HEAD), BF16),
             pltpu.VMEM((8, ROWS), F32),
             pltpu.VMEM((8, ROWS), F32),
             dma((9,)),
+            dma((3,)),
+            dma((GROUP,)),
             dma((GROUP,)),
             dma((levels, 2, 2)),
             dma((2, 2, 2)),
@@ -544,7 +595,7 @@
             dma,
         ],
         compiler_params=pltpu.CompilerParams(
-            collective_id=0, has_side_effects=True, vmem_limit_bytes=48 * 2**20
+            collective_id=0, has_side_effects=True, vmem_limit_bytes=VMEM_BYTES
         ),
     )(
         span_order[None],
@@ -559,9 +610,10 @@
     out, mk, mv, dev = pl.pallas_call(
         deliver,
         out_shape=shapes,
-        in_specs=[vmem] * 4,
+        in_specs=[hbm] * 4,
         out_specs=(hbm,) * 4,
-        scratch_shapes=[dma((4,))],
+        scratch_shapes=[pltpu.VMEM(a.shape, a.dtype) for a in shapes] + [dma((4,)), dma((4,))],
+        compiler_params=pltpu.CompilerParams(vmem_limit_bytes=VMEM_BYTES),
     )(*results)
     return out[None], mk[None], mv[None], dev
 

time: 98.3 us -> 86.8 us (0.88)
  the two profiles are of different devices: /device:TPU:1 before, /device:TPU:4 now
where the time goes in v3:
time: 86.8 us; the launch traced here: 86.6 us
  Pallas kernels  85.9 us (99%)
    pallas_call x1, Pallas kernels, body(): pl.pallas_call(functools.partial(kernel, levels), out_shape=shapes, in_sp...  84 us
    pallas_call x1, Pallas kernels, body(): pl.pallas_call(deliver, out_shape=shapes, in_specs=[hbm] * 4, out_specs=(...  1.98 us

profile of v3, /device:TPU:4, one launch (start us, length us, event | category | flops | bytes accessed | tf_op | source)
XLA Modules:
  0.0 86.6 jit_solution(10374426890152800697)
XLA Ops:
  0.6 84.0 %shard_map.111 = (bf16[128,2048]{1,0:T(8,128)(2,1)}, bf16[256,256]{1,0:T(8,128)(2,1)}, bf16[256,256]{1,0:T(8,128)(2,1)}, f32[1,128]{1,0:T(1,128)}) custom-call(s32[1,32]{1,0:T(1,128)} %bitcast.15, s32[1,32]{1,0:T(1,128)} %bitcast.16, s32[32,128]{1,0:T(8,128)} %sel_h.1, bf16[256,256]{1,0:T(8,128)(2,1)} %bitcast.11, bf16[256,256]{1,0:T(8,128)(2,1)} %bitcast.12, ...), custom_call_target="tpu_custom_call" | custom-call | tf_op jit(solution)/shard_map/pallas_call | solution.py:547
  84.6 2.0 %shard_map.112 = (bf16[128,2048]{1,0:T(8,128)(2,1)}, bf16[256,256]{1,0:T(8,128)(2,1)}, bf16[256,256]{1,0:T(8,128)(2,1)}, f32[1,128]{1,0:T(1,128)}) custom-call(bf16[128,2048]{1,0:T(8,128)(2,1)} %get-tuple-element.12.refs_0_, bf16[256,256]{1,0:T(8,128)(2,1)} %get-tuple-element.13.refs_1_, bf16[256,256]{1,0:T(8,128)(2,1)} %get-tuple-element.14.refs_2_, ...), custom_call_target="tpu_custom_call" | custom-call | tf_op jit(solution)/shard_map/pallas_call | solution.py:610

commit v4 on v3

--- a/solution.py
+++ b/solution.py
@@ -216,15 +216,15 @@
 
     keep_mine = kept_rows(my_sel, my_live)[:KEPT]
     for kv, cache in enumerate((k_ref, v_ref)):
+        kept[0, kv, 0, 0:KEPT, :] = dot(keep_mine, cache[:, pl.ds(mine_at, HEAD)]).astype(BF16)
+    for direction in range(2):
+        ring(direction, 0, 0, 1, 1).start()
+    for kv, cache in enumerate((k_ref, v_ref)):
         away[kv] = dot(keep_mine, cache[:, pl.ds(away_at, HEAD)]).astype(BF16)
     across = send(
         away, kept_of(0, 1), away_send.at[1], block_recv.at[0, 1, 1], {"mirror": partner}
     )
     across.start()
-    for kv, cache in enumerate((k_ref, v_ref)):
-        kept[0, kv, 0, 0:KEPT, :] = dot(keep_mine, cache[:, pl.ds(mine_at, HEAD)]).astype(BF16)
-    for direction in range(2):
-        ring(direction, 0, 0, 1, 1).start()
 
     def ask(g):
         return send(
@@ -243,6 +243,19 @@
     total[...] = jnp.zeros_like(total)
     top[...] = jnp.full_like(top, LOW)
     kept[:, 1, :, KEPT:, :] = jnp.zeros((levels, 2, TOKENS - KEPT, HEAD), BF16)
+
+    def relay(unit, kinds=(0, 1)):
+        for kind in kinds:
+            for direction in range(2):
+                arrived(unit, direction, kind)
+
+                @pl.when(unit < last - 2)
+                def _():
+                    ring(direction, unit, direction, kind, unit + 2).start()
+
+                @pl.when(unit >= last - 2)
+                def _():
+                    far(direction, (unit + 1) % 2, kind, unit).start()
 
     counts_f = counts_v[...].astype(F32)
     c_at, s_at = iota((spans, spans), 0), iota((spans, spans), 1)
@@ -265,6 +278,7 @@
         same = jnp.where(span_at == at, 1.0, 0.0)
         token_fresh[o] = jnp.where(iota((spans, ROWS), 1) < end, same * sel_row, FAR)
 
+    relay(1, (0,))
     across.wait_send()
     for g in range(GROUP):
         ask(g).start()
@@ -321,19 +335,6 @@
         ]
         attend(o, (first, second), *both)
 
-    def relay(unit):
-        for kind in range(2):
-            for direction in range(2):
-                arrived(unit, direction, kind)
-
-                @pl.when(unit < last - 2)
-                def _():
-                    ring(direction, unit, direction, kind, unit + 2).start()
-
-                @pl.when(unit >= last - 2)
-                def _():
-                    far(direction, (unit + 1) % 2, kind, unit).start()
-
     def find(s, found):
         return tuple(
             jnp.where(order_s[0, s] == span, s, slot) for span, slot in zip((me, partner), found)
@@ -341,37 +342,50 @@
 
     my_slot, partner_slot = lax.fori_loop(0, spans, find, (0, 0))
 
-    def early(i, carry):
-        for at, unit in ((0, 1), (1, 2), (3, 3)):
-            @pl.when(i == at)
-            def _():
-                relay(unit)
-
-        @pl.when(i == 2)
+    def own_first(unit, carry):
+        @pl.when(unit == 1)
         def _():
-            for g in range(GROUP):
-                ask(g).wait_recv()
-
-        o = jnp.where((i >= 2) & (i <= 4), 1, 0)
-        absorb(jnp.where(i < 2, i, jnp.where(i < 5, i - 2, 2)), o)
+            relay(1, (1,))
+
+        @pl.when(unit == 2)
+        def _():
+            relay(2)
+
+        absorb(unit, 0)
         return carry
 
-    lax.fori_loop(0, 6, early, 0)
+    lax.fori_loop(0, 3, own_first, 0)
+    for g in range(GROUP):
+        ask(g).wait_recv()
+    absorb(0, 1)
+
+    def behind(unit, carry):
+        relay(unit)
+        absorb(unit, 0)
+        absorb(unit - 2, 1)
+        return carry
+
+    def gaining(unit, carry):
+        relay(unit)
+        absorb(unit, 0)
+        absorb(2 * unit - 7, 1)
+        absorb(2 * unit - 6, 1)
+        return carry
 
     def step(unit, carry):
         relay(unit)
         for o in (1, 0):
-            absorb(unit - 1, o)
+            absorb(unit, o)
         return carry
 
-    lax.fori_loop(4, last - 1, step, 0)
+    gained = min(7, last - 1)
+    lax.fori_loop(3, 5, behind, 0)
+    lax.fori_loop(5, gained, gaining, 0)
+    lax.fori_loop(gained, last - 1, step, 0)
     relay(last - 1)
-
-    def late(unit, carry):
+    seen_by_partner = last - 1 if gained == 7 else 2 * gained - 7
+    for unit in range(seen_by_partner, last):
         absorb(unit, 1)
-        return carry
-
-    lax.fori_loop(last - 2, last, late, 0)
 
     def out_columns(g):
         return out_h.at[:, pl.ds(pl.multiple_of(mine_q + g * HEAD, HEAD), HEAD)]
@@ -383,9 +397,9 @@
             answer_send.at[g], answer_recv.at[g], {"mirror": partner},
         )
 
-    def far_half(half, after=None):
+    def far_half(half, o, after=None):
         attend(
-            1,
+            o,
             (((z + half_way) % levels) * 2 + (y + half) % 2,),
             *[(kept[last, kv, half], fresh[last, kv, half]) for kv in range(2)],
             after=after,
@@ -397,7 +411,7 @@
 
     far_arrived(0, 0)
     far_arrived(0, 1)
-    far_half(0)
+    far_half(0, 1)
     far_arrived(1, 0)
 
     def where_is(slot):
@@ -414,6 +428,7 @@
         rows_out[kv] = fresh[unit, kv, side]
     hand = send(rows_out, rows_in, rows_send, rows_recv, {"mirror": partner})
     hand.start()
+    far_half(0, 0)
 
     far_arrived(1, 1)
     partner_live = counts_s[0, partner].astype(F32)
@@ -428,7 +443,19 @@
             answer[g] = live_only(result[i * ROWS:(i + 1) * ROWS], partner_live)
             reply(g).start()
 
-    far_half(1, give_back)
+    far_half(1, 1, give_back)
+
+    def keep(g):
+        return pltpu.make_async_copy(own_out.at[g], out_columns(g), own_sem.at[g])
+
+    def keep_tile(t, result):
+        for i in range(TILE // ROWS):
+            g = t * (TILE // ROWS) + i
+            own_out[g] = live_only(result[i * ROWS:(i + 1) * ROWS], own_live)
+            keep(g).start()
+
+    absorb(last - 1, 0)
+    far_half(1, 0, keep_tile)
 
     unit, side = where_is(my_slot)
     match = (iota((TOKENS, ROWS), 0) == my_sel) & (iota((TOKENS, ROWS), 1) < my_live)
@@ -468,18 +495,6 @@
     for store in stores:
         store.start()
 
-    def own_rest(unit, carry):
-        absorb(unit, 0)
-        return carry
-
-    lax.fori_loop(last - 2, levels, own_rest, 0)
-    def keep(g):
-        return pltpu.make_async_copy(own_out.at[g], out_columns(g), own_sem.at[g])
-
-    for g in range(GROUP):
-        rows = slice(g * ROWS, (g + 1) * ROWS)
-        own_out[g] = live_only(acc[0, rows, :] / total[0, rows, :], own_live)
-        keep(g).start()
     swap.wait_recv()
     mean = (gap_mine[:1] + gap_other[:1]) / (4.0 * HEAD)
     dev_ref[...] = jnp.where(iota((1, ROWS), 1) < my_live, mean, 0.0)

time: 86.8 us -> 83.9 us (0.967)
  the two profiles are of different devices: /device:TPU:4 before, /device:TPU:1 now
where the time goes in v4:
time: 83.9 us; the launch traced here: 83.7 us
  Pallas kernels  82.9 us (99%)
    pallas_call x1, Pallas kernels, body(): pl.pallas_call(functools.partial(kernel, levels), out_shape=shapes, in_sp...  80.9 us
    pallas_call x1, Pallas kernels, body(): pl.pallas_call(deliver, out_shape=shapes, in_specs=[hbm] * 4, out_specs=(...  1.98 us

profile of v4, /device:TPU:1, one launch (start us, length us, event | category | flops | bytes accessed | tf_op | source)
XLA Modules:
  0.0 83.7 jit_solution(11558260052642261990)
XLA Ops:
  0.6 80.9 %shard_map.111 = (bf16[128,2048]{1,0:T(8,128)(2,1)}, bf16[256,256]{1,0:T(8,128)(2,1)}, bf16[256,256]{1,0:T(8,128)(2,1)}, f32[1,128]{1,0:T(1,128)}) custom-call(s32[1,32]{1,0:T(1,128)} %bitcast.15, s32[1,32]{1,0:T(1,128)} %bitcast.16, s32[32,128]{1,0:T(8,128)} %sel_h.1, bf16[256,256]{1,0:T(8,128)(2,1)} %bitcast.11, bf16[256,256]{1,0:T(8,128)(2,1)} %bitcast.12, ...), custom_call_target="tpu_custom_call" | custom-call | tf_op jit(solution)/shard_map/pallas_call | solution.py:562
  81.6 2.0 %shard_map.112 = (bf16[128,2048]{1,0:T(8,128)(2,1)}, bf16[256,256]{1,0:T(8,128)(2,1)}, bf16[256,256]{1,0:T(8,128)(2,1)}, f32[1,128]{1,0:T(1,128)}) custom-call(bf16[128,2048]{1,0:T(8,128)(2,1)} %get-tuple-element.12.refs_0_, bf16[256,256]{1,0:T(8,128)(2,1)} %get-tuple-element.13.refs_1_, bf16[256,256]{1,0:T(8,128)(2,1)} %get-tuple-element.14.refs_2_, ...), custom_call_target="tpu_custom_call" | custom-call | tf_op jit(solution)/shard_map/pallas_call | solution.py:625
